TPU v7x, 128 devices: a whole 4x4x4 slice. The times are simulated.
128 devices in a mesh: gx: 8 (over x, core), gy: 16 (over y, z).
Axes of the slice: x: 4, y: 4, z: 4, core: 2. Of those that a mesh axis runs over, the one named last changes fastest.
Arguments:
- ocean_state: float32 [4, 16, 768, 2304], P(None, None, 'gy', 'gx'), may hold values from -8 to 8, as said below
- layer_thickness: float32 [16], replicated, may hold values from 0.05 to 0.3
- vertical_mixing: float32 [768, 2304], P('gy', 'gx'), may hold values from 0.1 to 10
- damping: float32 [768, 2304], P('gy', 'gx'), may hold values from 0.02 to 3
- ocean_blocks: int32 [32, 64], replicated, may hold values from 0 to 1, as said below
Outputs:
- tracer_next: float32 [2, 16, 768, 2304], P(None, None, 'gy', 'gx')
- surface_height: float32 [768, 2304], P('gy', 'gx')
Inputs may be any that keep to these rules, and one draw needn't show every extreme that they name: `ocean_state`: the first two components are temperature and salinity, the last two the eastward and northward velocity. `ocean_blocks`: each device's patch of 2 x 8 blocks (latitude rows from j * 2, longitude columns from i * 8, for gy index j and gx index i) holds 3 to 16 ocean blocks; in every draw some patch and the patches on both sides of it along latitude are wholly ocean, and a patch next to that run of three along latitude holds exactly 3.
All inputs are finite; a program needn't handle non-finite values.
Results may differ from a plain program's by a relative error of at most 0.0003.
Values sent between devices are 32-bit elements; how exact they have to be, the bound alone decides.
A program may use at most 64 MiB of HBM per device.

v0:
```python
import functools

import jax
import jax.numpy as jnp
from jax import lax
from jax.experimental import pallas as pl
from jax.experimental.pallas import tpu as pltpu
from jax.sharding import PartitionSpec as P

BLAT = 24
BLON = 36
LEV = 16
ROWS = 48
COLS = 288
WIDE = 384
EXT = 56
TILES = ROWS // 8

f32 = jnp.float32
MESH = pl.DeviceIdType.MESH

NORTH, SOUTH, EAST, WEST = (0, 1), (0, -1), (1, 0), (-1, 0)
DIAGONAL = ((1, 1), (-1, 1), (1, -1), (-1, -1))


def iota(shape, dim):
    return lax.broadcasted_iota(jnp.int32, shape, dim)


def padded(value):
    return jnp.concatenate([value, jnp.zeros((value.shape[0], WIDE - COLS), f32)], axis=1)


def east_of(value):
    return pltpu.roll(value, WIDE - 1, 1)


def west_of(value):
    return pltpu.roll(value, 1, 1)


def inverse(value):
    guess = pl.reciprocal(value, approx=True)
    return guess * (2.0 - value * guess)


def row_pack(low, high):
    return jnp.where(iota(low.shape, 0) < 4, low, high)


def column_pack(first, last):
    lane = iota(first.shape, 1)
    low = pltpu.roll(first, 32, 1)
    high = pltpu.roll(last, 96, 1)
    return jnp.where(
        (lane >= 32) & (lane < 36), low, jnp.where(lane >= 124, high, 0.0)
    )


def kernel(
    nx,
    ny,
    ocean,
    thick,
    mixing,
    damping,
    blocks,
    tracer_out,
    surface_out,
    state,
    h,
    mix,
    damp,
    blk,
    mask,
    level_inv,
    flat,
    send_rows,
    send_heat,
    recv_rows,
    recv_heat,
    send_cols,
    recv_cols,
    send_corner,
    recv_corner,
    recv_side,
    flux_lon,
    flux_north,
    flux_prev,
    ratio,
    scale,
    weigh,
    basis,
    halo_rows,
    halo_cols,
    halo_corner,
    recv_halo_rows,
    recv_halo_cols,
    recv_halo_corner,
    message,
    first_sum,
    second_message,
    second_sum,
    load_sem,
    small_sem,
    send_sem,
    recv_sem,
    halo_send_sem,
    halo_recv_sem,
    sum_send_sem,
    sum_recv_sem,
):
    gx = lax.axis_index("gx")
    gy = lax.axis_index("gy")

    def device(step):
        return {"gx": lax.rem(gx + step[0] + nx, nx), "gy": lax.rem(gy + step[1] + ny, ny)}

    def greet(step):
        pl.semaphore_signal(barrier, inc=1, device_id=device(step), device_id_type=MESH)

    small = [
        pltpu.make_async_copy(blocks, blk, small_sem.at[0]),
        pltpu.make_async_copy(thick, h, small_sem.at[1]),
        pltpu.make_async_copy(damping, damp, small_sem.at[2]),
        pltpu.make_async_copy(mixing, mix, small_sem.at[3]),
    ]
    group = LEV // 4

    def load(index):
        levels = pl.ds(group * index, group)
        return pltpu.make_async_copy(
            ocean.at[:, levels, :, :], state.at[:, levels, :, :], load_sem.at[index]
        )

    for copy in small[:3] + [load(index) for index in range(4)] + small[3:]:
        copy.start()

    barrier = pltpu.get_barrier_semaphore()
    for step in DIAGONAL:
        greet(step)
    pl.loop(1, nx)(lambda d: greet((d, 0)))
    pl.loop(1, ny)(lambda d: greet((0, d)))
    partners = len(DIAGONAL) + nx - 1 + ny - 1

    block_rows, block_cols = blk.shape
    small[0].wait()
    row = iota((EXT, block_rows), 0)
    row = gy * ROWS + jnp.where(row < ROWS + 4, row, row - EXT)
    edge = iota((EXT, block_rows), 1) * BLAT
    pick_rows = jnp.where((row >= edge) & (row < edge + BLAT), 1.0, 0.0)
    lane = iota((block_cols, WIDE), 1)
    total = block_cols * BLON
    col = gx * COLS + jnp.where(lane < COLS + 4, lane, lane - WIDE)
    col = jnp.where(col < 0, col + total, jnp.where(col >= total, col - total, col))
    edge = iota((block_cols, WIDE), 0) * BLON
    inside = (lane < COLS + 4) | (lane >= WIDE - 4)
    pick_cols = jnp.where(inside & (col >= edge) & (col < edge + BLON), 1.0, 0.0)
    coarse = jnp.dot(pick_rows, blk[...].astype(f32), preferred_element_type=f32)
    mask[...] = jnp.dot(coarse, pick_cols, preferred_element_type=f32)

    small[1].wait()
    level_inv[...] = jnp.zeros(level_inv.shape, f32)

    @pl.loop(1, LEV)
    def _(k):
        level_inv[pl.ds(k, 1), :] = 1.0 / jnp.full((1, WIDE), h[k - 1] + h[k], f32)


    small[2].wait()
    damp_low = padded(damp[0:8, :])
    damp_high = padded(damp[ROWS - 8 : ROWS, :])
    damp_rows = row_pack(damp_low, damp_high)
    for side in range(2):
        send_rows[side, 32:40, :] = damp_rows
    damp_all = padded(damp[...])
    send_cols[ROWS : 2 * ROWS, :] = column_pack(damp_all[:, 0:128], damp_all[:, 256:384])
    send_corner[16:24, :] = column_pack(damp_rows[:, 0:128], damp_rows[:, 256:384])

    def remote(source, target, index, step, sends=send_sem, recvs=recv_sem):
        return pltpu.make_async_remote_copy(
            src_ref=source,
            dst_ref=target,
            send_sem=sends.at[index],
            recv_sem=recvs.at[index],
            device_id=device(step),
            device_id_type=MESH,
        )

    sub = iota((8, WIDE), 0)

    def next_row(i):
        return jnp.minimum(8 * i + 8, ROWS - 1)

    tiles = [pl.ds(8 * i, 8) for i in range(TILES)]
    flat[...] = jnp.zeros(flat.shape, f32)

    def turned_up(values):
        turned = [pltpu.roll(value, 7, 0) for value in values]
        return [
            jnp.where(sub == 7, turned[(i + 1) % TILES], turned[i]) for i in range(TILES)
        ]

    @pl.loop(0, LEV // 2)
    def _(pair):
        @pl.when(lax.rem(pair, group // 2) == 0)
        def _():
            load(pair // (group // 2)).wait()

        sums = None
        for k in (2 * pair, 2 * pair + 1):
            s = [
                padded(state[0, k, rows, :] - 0.5 * state[1, k, rows, :]) * mask[rows, :] * h[k]
                for rows in tiles
            ]
            v = [padded(state[3, k, rows, :]) * mask[rows, :] for rows in tiles]
            s_north, v_north = turned_up(s), turned_up(v)
            found = []
            for i, rows in enumerate(tiles):
                u = padded(state[2, k, rows, :]) * mask[rows, :]
                found.append(
                    (
                        s[i],
                        (u + east_of(u)) * (s[i] + east_of(s[i])),
                        (v[i] + v_north[i]) * (s[i] + s_north[i]),
                    )
                )
            if sums is None:
                sums = found
            else:
                sums = [[a + b for a, b in zip(x, y)] for x, y in zip(sums, found)]
        for i, rows in enumerate(tiles):
            for part in range(3):
                flat[part, rows, :] += sums[i][part]

    first_round = []
    for side, (edge_row, step) in enumerate(((ROWS - 1, NORTH), (0, SOUTH))):
        edge_mask = mask[edge_row : edge_row + 1, :]
        heat = padded(state[0, :, edge_row, :]) * edge_mask
        salt = padded(state[1, :, edge_row, :]) * edge_mask
        send_heat[side] = heat
        send_rows[side, 0:16, :] = heat - 0.5 * salt
        send_rows[side, 16:32, :] = padded(state[3, :, edge_row, :]) * edge_mask
        first_round.append(remote(send_rows.at[side], recv_rows.at[side], side, step))

    pl.semaphore_wait(barrier, partners)
    for copy in first_round:
        copy.start()

    lane128 = iota((8, 128), 1)

    @pl.loop(0, TILES)
    def _(i):
        rows = pl.ds(pl.multiple_of(8 * i, 8), 8)
        edge_mask = jnp.where(lane128 == 31, mask[rows, 256:384], mask[rows, 0:128])
        acc_west = jnp.zeros((8, 128), f32)
        acc_east = jnp.zeros((8, 128), f32)
        for field, base in ((0, 0), (1, 16), (2, 64)):
            for k in range(LEV):
                first = state[field, k, rows, 0:128]
                last = jnp.concatenate(
                    [state[field, k, rows, 256:COLS], jnp.zeros((8, WIDE - COLS), f32)], axis=1
                )
                merged = jnp.where(lane128 == 31, last, first)
                turned = pltpu.roll(merged, base + k, 1) if base + k else merged
                acc_west = jnp.where(lane128 == base + k, turned, acc_west)
                acc_east = jnp.where(lane128 == base + k + 31, turned, acc_east)
        west_mask = jnp.broadcast_to(edge_mask[:, 0:1], (8, 128))
        east_mask = jnp.broadcast_to(edge_mask[:, 31:32], (8, 128))
        send_cols[rows, :] = acc_west * west_mask + pltpu.roll(acc_east, 1, 1) * east_mask


    compact = jnp.zeros((8, 128), f32)
    for side in range(2):
        for part in range(4):
            j = 4 * side + part
            rows = pl.ds(8 * part, 8)
            first = pltpu.roll(send_rows[side, rows, 0:128], 16 * j, 1)
            last = pltpu.roll(send_rows[side, rows, 256:384], (16 * j - 24) % 128, 1)
            inside = lane128 // 16 == j
            compact = jnp.where(inside & (lane128 % 16 < 4), first, compact)
            compact = jnp.where(
                inside & (lane128 % 16 >= 4) & (lane128 % 16 < 8), last, compact
            )
    send_corner[0:8, :] = compact
    send_cols[2 * ROWS :, :] = compact
    send_corner[8:16, :] = row_pack(send_cols[0:8, :], send_cols[ROWS - 8 : ROWS, :])

    second_round = []
    for side, step in enumerate((EAST, WEST)):
        second_round.append(remote(send_cols, recv_cols.at[side], 2 + side, step))
    for place, step in enumerate(DIAGONAL):
        second_round.append(remote(send_corner, recv_corner.at[place], 4 + place, step))
    for side, step in enumerate((NORTH, SOUTH)):
        second_round.append(
            remote(send_corner.at[pl.ds(8, 8)], recv_side.at[side], 10 + side, step)
        )
    for copy in second_round:
        copy.start()
    first_round = first_round + second_round

    lane_f = iota((ROWS, WIDE), 1)
    row_f = iota((ROWS, WIDE), 0)
    plain = flat[0]
    lon = 0.05 * flat[1] - 0.1 * (east_of(plain) - plain)
    lon = jnp.where(lane_f < COLS - 1, lon, 0.0)
    lat = 0.05 * flat[2] - 0.1 * (pltpu.roll(plain, ROWS - 1, 0) - plain)
    lat = jnp.where(row_f == ROWS - 1, 0.0, lat)
    start = plain - (lon - west_of(lon)) - (lat - pltpu.roll(lat, 1, 0))
    start = jnp.where(lane_f < COLS, start, 0.0)
    basis[1, 0:ROWS, :] = start
    packed_rows = row_pack(start[0:8, :], start[ROWS - 8 : ROWS, :])
    halo_rows[...] = packed_rows
    halo_cols[...] = column_pack(start[:, 0:128], start[:, 256:384])
    halo_corner[...] = column_pack(packed_rows[:, 0:128], packed_rows[:, 256:384])
    second_round = []
    for side, step in enumerate((NORTH, SOUTH)):
        second_round.append(
            remote(halo_rows, recv_halo_rows.at[side], side, step, halo_send_sem, halo_recv_sem)
        )
    for side, step in enumerate((EAST, WEST)):
        second_round.append(
            remote(halo_cols, recv_halo_cols.at[side], 2 + side, step, halo_send_sem, halo_recv_sem)
        )
    for place, step in enumerate(DIAGONAL):
        second_round.append(
            remote(
                halo_corner,
                recv_halo_corner.at[place],
                4 + place,
                step,
                halo_send_sem,
                halo_recv_sem,
            )
        )
    for copy in second_round:
        copy.start()
    heat_round = []
    for side, step in enumerate((NORTH, SOUTH)):
        copy = remote(send_heat.at[side], recv_heat.at[side], 8 + side, step)
        copy.start()
        heat_round.append(copy)

    for copy in first_round + second_round:
        copy.wait()

    def beside(north, south):
        return jnp.where(iota((8, 128), 0) < 4, north, south)

    own = jnp.concatenate([send_cols[0:ROWS, :], beside(recv_side[1], recv_side[0])], axis=0)
    from_east = jnp.concatenate(
        [recv_cols[1, 0:ROWS, :], beside(recv_corner[3, 8:16, :], recv_corner[1, 8:16, :])], axis=0
    )
    from_west = jnp.concatenate(
        [recv_cols[0, 0:ROWS, :], beside(recv_corner[2, 8:16, :], recv_corner[0, 8:16, :])], axis=0
    )
    lane_c = iota((EXT, 128), 1)
    is_east = (lane_c & 32) != 0
    other = jnp.where(is_east, pltpu.roll(from_east, 32, 1), pltpu.roll(from_west, 96, 1))
    both = own + other
    speed = pltpu.roll(both, 64, 1)
    speed = jnp.where((lane_c & 16) != 0, pltpu.roll(speed, 16, 1), speed)
    slope = jnp.where(is_east, 0.1, -0.1) * (other - own)
    through = 0.05 * speed * both - slope
    flux_lon[...] = through[0:ROWS, :]
    weight = jnp.zeros((1, 128), f32)
    lane_w = iota((1, 128), 1)
    for k in range(LEV):
        weight = jnp.where((lane_w & 15) == k, h[k], weight)
    weight = weight * jnp.where((lane_w & 16) != 0, -0.5, 1.0)
    weighed = through * weight
    side_west = jnp.sum(jnp.where(lane_c < 32, weighed, 0.0), axis=1, keepdims=True)
    side_east = jnp.sum(
        jnp.where(is_east & (lane_c < 64), weighed, 0.0), axis=1, keepdims=True
    )

    level_weight = jnp.zeros((LEV, WIDE), f32)
    level_row = iota((LEV, WIDE), 0)
    for k in range(LEV):
        level_weight = jnp.where(level_row == k, h[k], level_weight)
    exists = (
        jnp.where(gy < ny - 1, 1.0, 0.0).astype(f32),
        jnp.where(gy > 0, 1.0, 0.0).astype(f32),
    )

    def side_flux(mine, theirs, speeds, sign):
        return speeds * (mine + theirs) - (0.1 * sign) * (theirs - mine)

    side_lat = []
    speed_lat = []
    for side, sign in ((0, 1.0), (1, -1.0)):
        slot = 1 - side
        s_mine = send_rows[side, 0:16, :]
        s_theirs = recv_rows[slot, 0:16, :] * exists[side]
        speeds = 0.05 * (send_rows[side, 16:32, :] + recv_rows[slot, 16:32, :] * exists[side])
        speed_lat.append(speeds)
        flux = side_flux(s_mine, s_theirs, speeds, sign)
        side_lat.append(jnp.sum(flux * level_weight, axis=0, keepdims=True))

    is_first = (lane128 & 15) < 4
    is_north = lane128 < 64
    mine = jnp.where(is_first, recv_cols[1, 2 * ROWS :, :], recv_cols[0, 2 * ROWS :, :])
    theirs_north = jnp.where(is_first, recv_corner[3, 0:8, :], recv_corner[2, 0:8, :])
    theirs_south = jnp.where(is_first, recv_corner[1, 0:8, :], recv_corner[0, 0:8, :])
    theirs = pltpu.roll(
        jnp.where(is_north, theirs_south * exists[1], theirs_north * exists[0]), 64, 1
    )
    both = mine + theirs
    flux = 0.05 * pltpu.roll(both, 96, 1) * both - jnp.where(is_north, 0.1, -0.1) * (theirs - mine)
    flux = flux * jnp.where(
        (lane128 & 16) == 0, level_weight[0:8, 0:128], level_weight[8:16, 0:128]
    )
    flux = jnp.sum(flux, axis=0, keepdims=True)
    flux = flux + pltpu.roll(flux, 112, 1)
    for side in range(2):
        low = pltpu.roll(flux, 32 - 64 * side if side == 0 else 96, 1)
        high = pltpu.roll(flux, 120 if side == 0 else 56, 1)
        third = jnp.where(
            lane_w < 32, side_lat[side][:, 256:384], jnp.where(lane_w < 64, low, high)
        )
        side_lat[side] = jnp.concatenate([side_lat[side][:, 0:256], third], axis=1)

    def assemble(center, rows_in, cols_in, corner_in):
        lane8 = iota((8, 128), 1)
        lane48 = iota((ROWS, 128), 1)
        third = jnp.where(
            lane48 < 32, center[:, 256:384], jnp.where(lane48 < 64, cols_in(1), cols_in(0))
        )
        upper = jnp.concatenate([center[:, 0:256], third], axis=1)
        north_south = jnp.where(sub < 4, rows_in(1), rows_in(0))
        north = jnp.where(lane8 < 64, corner_in(3), corner_in(2))
        south = jnp.where(lane8 < 64, corner_in(1), corner_in(0))
        corner = jnp.where(iota((8, 128), 0) < 4, north, south)
        third = jnp.where(lane8 < 32, north_south[:, 256:384], corner)
        lower = jnp.concatenate([north_south[:, 0:256], third], axis=1)
        return jnp.concatenate([upper, lower], axis=0)

    damp_ext = assemble(
        damp_all,
        lambda slot: recv_rows[slot, 32:40, :],
        lambda slot: recv_cols[slot, ROWS : 2 * ROWS, :],
        lambda place: recv_corner[place, 16:24, :],
    )
    inv = mask[...] * inverse(6.0 + damp_ext)
    scale[...] = 1.5 * inv
    weigh[...] = jnp.where(iota((ROWS, WIDE), 1) < COLS, 6.0 + damp_all, 0.0)
    forcing = assemble(
        basis[1, 0:ROWS, :],
        lambda slot: recv_halo_rows[slot],
        lambda slot: recv_halo_cols[slot],
        lambda place: recv_halo_corner[place],
    )
    forcing = jnp.concatenate(
        [
            forcing[:, 0:128] + jnp.where(lane_c == 0, side_west, 0.0),
            forcing[:, 128:256],
            forcing[:, 256:384]
            + jnp.where(
                lane_c == 31,
                -side_east,
                jnp.where(lane_c == 32, side_east, jnp.where(lane_c == 127, -side_west, 0.0)),
            ),
        ],
        axis=1,
    )
    north, south = side_lat
    forcing = jnp.concatenate(
        [
            forcing[0:8, :] + jnp.where(sub == 0, south, 0.0),
            forcing[8:40, :],
            forcing[40:48, :] - jnp.where(sub == 7, north, 0.0),
            forcing[48:56, :]
            + jnp.where(sub == 0, north, jnp.where(sub == 7, -south, 0.0)),
        ],
        axis=0,
    )
    basis[0] = jnp.zeros((EXT, WIDE), f32)
    basis[1] = forcing * inv

    def folded(value):
        value = value[:, 0:128] + value[:, 128:256] + value[:, 256:384]
        return jnp.sum(value, axis=0, keepdims=True)

    @pl.loop(0, 4)
    def _(index):
        q = basis[index + 1]
        pair = east_of(q) + west_of(q)
        column = q + 0.5 * pair
        around = pair + pltpu.roll(column, EXT - 1, 0) + pltpu.roll(column, 1, 0)
        image = scale[...] * around - 0.5 * q
        later = jnp.where(index == 0, 0.0, 1.0)
        after = image + later * (image - basis[index])
        basis[index + 2] = after
        weighed = weigh[...] * q[0:ROWS, :]
        message[pl.ds(2 * index, 1), :] = folded(weighed * q[0:ROWS, :])
        message[pl.ds(2 * index + 1, 1), :] = folded(weighed * after[0:ROWS, :])

    def spread(source, target, count, along, mine, base):
        target[mine] = source[...]

        @pl.loop(1, count)
        def _(d):
            pltpu.make_async_remote_copy(
                src_ref=source,
                dst_ref=target.at[mine],
                send_sem=sum_send_sem.at[base],
                recv_sem=sum_recv_sem.at[base],
                device_id=device(along(d)),
                device_id_type=MESH,
            ).start()

    def gathered(target, count, base):
        part = target.at[pl.ds(0, count - 1)]
        done = pltpu.make_async_remote_copy(
            src_ref=part,
            dst_ref=part,
            send_sem=sum_send_sem.at[base],
            recv_sem=sum_recv_sem.at[base],
            device_id=device(EAST),
            device_id_type=MESH,
        )
        done.wait_recv()
        done.wait_send()
        return jnp.sum(target[...], axis=0)

    spread(message, first_sum, nx, lambda d: (d, 0), gx, 0)

    for copy in heat_round:
        copy.wait()
    for side, sign in ((0, 1.0), (1, -1.0)):
        slot = 1 - side
        target = flux_north if side == 0 else flux_prev
        heat_mine = send_heat[side]
        heat_theirs = recv_heat[slot] * exists[side]
        salt_mine = 2.0 * (heat_mine - send_rows[side, 0:16, :])
        salt_theirs = 2.0 * (heat_theirs - recv_rows[slot, 0:16, :] * exists[side])
        target[0:16, :] = side_flux(heat_mine, heat_theirs, speed_lat[side], sign)
        target[16:32, :] = side_flux(salt_mine, salt_theirs, speed_lat[side], sign)
    small[3].wait()

    edge_lane = (lane128 == 31) | (lane128 == 127)

    def mix_tile(i, _):
        rows = pl.ds(pl.multiple_of(8 * i, 8), 8)
        row = pl.ds(next_row(i), 1)
        here = mask[rows, :]
        beyond = mask[row, :]
        coefficient = padded(mix[rows, :])
        through = flux_lon[rows, :]
        use_north = (sub == 7) & (i == TILES - 1)

        def level(k, carry):
            ratio_low, heat_low, salt_low = carry
            u = padded(state[2, k, rows, :]) * here
            v = padded(state[3, k, rows, :]) * here
            v_row = padded(state[3, k, row, :]) * beyond
            v_north = jnp.where(sub == 7, v_row, pltpu.roll(v, 7, 0))
            u_pair = 0.05 * (u + east_of(u))
            v_pair = 0.05 * (v + v_north)
            lon_far, lon_near = u_pair - 0.1, u_pair + 0.1
            lat_far, lat_near = v_pair - 0.1, v_pair + 0.1
            below = coefficient * level_inv[pl.ds(k, 1), :]
            above = coefficient * level_inv[pl.ds(k + 1, 1), :]
            pivot = inverse(h[k] + above + below * (1.0 - ratio_low))
            ratio_now = above * pivot
            ratio[k] = ratio_now
            found = []
            for tracer, low in ((0, heat_low), (1, salt_low)):
                plane = tracer * LEV + k
                c = padded(state[tracer, k, rows, :]) * here
                c_row = padded(state[tracer, k, row, :]) * beyond
                c_north = jnp.where(sub == 7, c_row, pltpu.roll(c, 7, 0))
                lon = lon_far * east_of(c) + lon_near * c
                turned = pltpu.roll(through, 127 - plane, 1)
                lon = jnp.concatenate(
                    [lon[:, 0:256], jnp.where(edge_lane, turned, lon[:, 256:384])], axis=1
                )
                lat = lat_far * c_north + lat_near * c
                lat = jnp.where(use_north, flux_north[pl.ds(plane, 1), :], lat)
                lat_south = jnp.where(
                    sub == 0, flux_prev[pl.ds(plane, 1), :], pltpu.roll(lat, 1, 0)
                )
                flux_prev[pl.ds(plane, 1), :] = lat[7:8, :]
                advected = here * (c - (lon - west_of(lon)) - (lat - lat_south))
                value = (h[k] * advected + below * low) * pivot
                tracer_out[tracer, k, rows, :] = value[:, 0:COLS]
                found.append(value)
            return ratio_now, found[0], found[1]

        zero = jnp.zeros((8, WIDE), f32)
        _, heat, salt = lax.fori_loop(0, LEV, level, (zero, zero, zero), unroll=4)

        def back(step, carry):
            k = LEV - 2 - step
            heat_up, salt_up = carry
            share = ratio[k][:, 0:COLS]
            heat_up = tracer_out[0, k, rows, :] + share * heat_up
            salt_up = tracer_out[1, k, rows, :] + share * salt_up
            tracer_out[0, k, rows, :] = heat_up
            tracer_out[1, k, rows, :] = salt_up
            return heat_up, salt_up

        lax.fori_loop(0, LEV - 1, back, (heat[:, 0:COLS], salt[:, 0:COLS]), unroll=5)
        return 0

    lax.fori_loop(0, 2, mix_tile, 0)
    second_message[...] = gathered(first_sum, nx, 0)
    spread(second_message, second_sum, ny, lambda d: (0, d), gy, 1)
    lax.fori_loop(2, TILES, mix_tile, 0)
    sums = gathered(second_sum, ny, 1)

    sums = jnp.broadcast_to(jnp.sum(sums, axis=1, keepdims=True), (8, 128))
    dots = [sums[i : i + 1, :] for i in range(8)]
    moment = dots[0:2] + [2.0 * dots[i] - dots[i % 2] for i in range(2, 8)]

    def gram(i, j):
        return 0.5 * (moment[i + j] + moment[abs(i - j)])

    lower = {}
    pivots = []
    right = []
    for i in range(4):
        value = moment[i]
        for j in range(i + 1):
            entry = gram(i, j) - 0.5 * (gram(j, i + 1) + gram(j, abs(i - 1)))
            for k in range(j):
                entry = entry - lower[i, k] * lower[j, k] * pivots[k]
            if j < i:
                lower[i, j] = entry / pivots[j]
                value = value - lower[i, j] * right[j]
            else:
                pivots.append(entry)
        right.append(value)
    solved = [None] * 4
    for i in range(3, -1, -1):
        value = right[i] / pivots[i]
        for j in range(i + 1, 4):
            value = value - lower[j, i] * solved[j]
        solved[i] = value
    surface = None
    for i in range(4):
        factor = 1.5 * solved[i]
        factor = jnp.concatenate([factor, factor, factor], axis=1)
        term = factor * basis[i + 1, 0:ROWS, :]
        surface = term if surface is None else surface + term
    surface_out[...] = surface[:, 0:COLS]


def store(tracer, surface, tracer_out, surface_out, sems):
    copies = [pltpu.make_async_copy(surface, surface_out, sems.at[8])]
    for index in range(8):
        levels = pl.ds(4 * (index % 4), 4)
        copies.append(
            pltpu.make_async_copy(
                tracer.at[index // 4, levels], tracer_out.at[index // 4, levels], sems.at[index]
            )
        )
    for copy in copies:
        copy.start()
    for copy in copies:
        copy.wait()


def scratch(nx, ny):
    vmem = lambda *shape: pltpu.VMEM(shape, f32)
    dma = pltpu.SemaphoreType.DMA
    return [
        vmem(4, LEV, ROWS, COLS),
        pltpu.SMEM((LEV,), f32),
        vmem(ROWS, COLS),
        vmem(ROWS, COLS),
        None,
        vmem(EXT, WIDE),
        vmem(24, WIDE),
        vmem(3, ROWS, WIDE),
        vmem(2, 40, WIDE),
        vmem(2, LEV, WIDE),
        vmem(2, 40, WIDE),
        vmem(2, LEV, WIDE),
        vmem(2 * ROWS + 8, 128),
        vmem(2, 2 * ROWS + 8, 128),
        vmem(24, 128),
        vmem(4, 24, 128),
        vmem(2, 8, 128),
        vmem(ROWS, 128),
        vmem(2 * LEV, WIDE),
        vmem(2 * LEV, WIDE),
        vmem(LEV, 8, WIDE),
        vmem(EXT, WIDE),
        vmem(ROWS, WIDE),
        vmem(6, EXT, WIDE),
        vmem(8, WIDE),
        vmem(ROWS, 128),
        vmem(8, 128),
        vmem(2, 8, WIDE),
        vmem(2, ROWS, 128),
        vmem(4, 8, 128),
        vmem(8, 128),
        vmem(nx, 8, 128),
        vmem(8, 128),
        vmem(ny, 8, 128),
        dma((4,)),
        dma((4,)),
        dma((12,)),
        dma((12,)),
        dma((8,)),
        dma((8,)),
        dma((2,)),
        dma((2,)),
    ]


def solution(mesh):
    nx, ny = mesh.shape["gx"], mesh.shape["gy"]

    def body(ocean_state, layer_thickness, vertical_mixing, damping, ocean_blocks):
        shapes = scratch(nx, ny)
        shapes[4] = pltpu.VMEM(ocean_blocks.shape, jnp.int32)
        call = pl.pallas_call(
            functools.partial(kernel, nx, ny),
            out_shape=[
                pltpu.VMEM((2, LEV, ROWS, COLS), f32),
                pltpu.VMEM((ROWS, COLS), f32),
            ],
            in_specs=[pl.BlockSpec(memory_space=pltpu.HBM)] * 5,
            out_specs=[pl.BlockSpec(memory_space=pltpu.VMEM)] * 2,
            scratch_shapes=shapes,
            compiler_params=pltpu.CompilerParams(
                collective_id=0, has_side_effects=True, vmem_limit_bytes=32 * 1024 * 1024
            ),
        )
        operands = [
            pltpu.with_memory_space_constraint(operand, pltpu.HBM)
            for operand in (ocean_state, layer_thickness, vertical_mixing, damping, ocean_blocks)
        ]
        tracer, surface = call(*operands)
        return tuple(
            pl.pallas_call(
                store,
                out_shape=[
                    jax.ShapeDtypeStruct((2, LEV, ROWS, COLS), f32),
                    jax.ShapeDtypeStruct((ROWS, COLS), f32),
                ],
                in_specs=[pl.BlockSpec(memory_space=pltpu.VMEM)] * 2,
                out_specs=[pl.BlockSpec(memory_space=pltpu.HBM)] * 2,
                scratch_shapes=[pltpu.SemaphoreType.DMA((9,))],
                compiler_params=pltpu.CompilerParams(vmem_limit_bytes=16 * 1024 * 1024),
            )(tracer, surface)
        )

    def wrapped(*args):
        with jax.sharding.use_abstract_mesh(mesh.abstract_mesh):
            return jax.shard_map(
                body,
                mesh=mesh,
                in_specs=(P(None, None, "gy", "gx"), P(), P("gy", "gx"), P("gy", "gx"), P()),
                out_specs=(P(None, None, "gy", "gx"), P("gy", "gx")),
                check_vma=False,
            )(*args)

    return wrapped
```

profile of v0, /device:TPU:1, one launch (start us, length us, event | category | flops | bytes accessed | tf_op | source)
XLA Modules:
  0.0 26.7 jit_solution(7346211589568369059)
XLA Ops:
  0.6 24.6 %shard_map.68 = (f32[2,16,48,288]{3,2,1,0:T(8,128)S(1)}, f32[48,288]{1,0:T(8,128)S(1)}) custom-call(f32[4,16,48,288]{3,2,1,0:T(8,128)} %ocean.1, f32[16]{0:T(128)} %thick.1, f32[48,288]{1,0:T(8,128)} %mixing.1, f32[48,288]{1,0:T(8,128)} %damping.1, s32[32,64]{1,0:T(8,128)} %blocks.1), custom_call_target="tpu_custom_call" | custom-call | tf_op jit(solution)/shard_map/pallas_call | solution.py:736
  25.3 1.5 %shard_map.69 = (f32[2,16,48,288]{3,2,1,0:T(8,128)}, f32[48,288]{1,0:T(8,128)}) custom-call(f32[2,16,48,288]{3,2,1,0:T(8,128)S(1)} %get-tuple-element.4.tracer, f32[48,288]{1,0:T(8,128)S(1)} %get-tuple-element.5.surface), custom_call_target="tpu_custom_call" | custom-call | tf_op jit(solution)/shard_map/pallas_call | solution.py:738
where the time goes:
time: 26.9 us; the launch traced here: 26.7 us
  Pallas kernels  26.1 us (97%)
  between operations  0.64 us (2%)
    pallas_call x1, Pallas kernels, body(): tracer, surface = call(*operands)  24.6 us
    pallas_call x1, Pallas kernels, body(): pl.pallas_call(store, out_shape=[jax.ShapeDtypeStruct((2, LEV, ROWS, COLS...  1.5 us

commit v1 on v0

--- a/solution.py
+++ b/solution.py
@@ -75,6 +75,7 @@
     mask,
     level_inv,
     flat,
+    ends,
     send_rows,
     send_heat,
     recv_rows,
@@ -160,13 +161,6 @@
     mask[...] = jnp.dot(coarse, pick_cols, preferred_element_type=f32)
 
     small[1].wait()
-    level_inv[...] = jnp.zeros(level_inv.shape, f32)
-
-    @pl.loop(1, LEV)
-    def _(k):
-        level_inv[pl.ds(k, 1), :] = 1.0 / jnp.full((1, WIDE), h[k - 1] + h[k], f32)
-
-
     small[2].wait()
     damp_low = padded(damp[0:8, :])
     damp_high = padded(damp[ROWS - 8 : ROWS, :])
@@ -188,12 +182,33 @@
         )
 
     sub = iota((8, WIDE), 0)
+    lane128 = iota((8, 128), 1)
 
     def next_row(i):
         return jnp.minimum(8 * i + 8, ROWS - 1)
 
     tiles = [pl.ds(8 * i, 8) for i in range(TILES)]
     flat[...] = jnp.zeros(flat.shape, f32)
+    ends[...] = jnp.zeros(ends.shape, f32)
+    end_mask = [
+        jnp.where(lane128 == 31, mask[rows, 256:384], mask[rows, 0:128]) for rows in tiles
+    ]
+
+    def pack_ends(pair):
+        for i, rows in enumerate(tiles):
+            west, east = ends[0, rows, :], ends[1, rows, :]
+            for k in (2 * pair, 2 * pair + 1):
+                for field, base in ((0, 0), (1, 16), (2, 64)):
+                    last = jnp.concatenate(
+                        [state[field, k, rows, 256:COLS], jnp.zeros((8, WIDE - COLS), f32)], axis=1
+                    )
+                    both = jnp.where(lane128 == 31, last, state[field, k, rows, 0:128])
+                    both = pltpu.roll(both * end_mask[i], base + k, 1)
+                    west = jnp.where(lane128 == base + k, both, west)
+                    east = jnp.where(lane128 == base + k + 31, both, east)
+            ends[0, rows, :] = west
+            ends[1, rows, :] = east
+
 
     def turned_up(values):
         turned = [pltpu.roll(value, 7, 0) for value in values]
@@ -232,6 +247,7 @@
         for i, rows in enumerate(tiles):
             for part in range(3):
                 flat[part, rows, :] += sums[i][part]
+        pack_ends(pair)
 
     first_round = []
     for side, (edge_row, step) in enumerate(((ROWS - 1, NORTH), (0, SOUTH))):
@@ -247,28 +263,7 @@
     for copy in first_round:
         copy.start()
 
-    lane128 = iota((8, 128), 1)
-
-    @pl.loop(0, TILES)
-    def _(i):
-        rows = pl.ds(pl.multiple_of(8 * i, 8), 8)
-        edge_mask = jnp.where(lane128 == 31, mask[rows, 256:384], mask[rows, 0:128])
-        acc_west = jnp.zeros((8, 128), f32)
-        acc_east = jnp.zeros((8, 128), f32)
-        for field, base in ((0, 0), (1, 16), (2, 64)):
-            for k in range(LEV):
-                first = state[field, k, rows, 0:128]
-                last = jnp.concatenate(
-                    [state[field, k, rows, 256:COLS], jnp.zeros((8, WIDE - COLS), f32)], axis=1
-                )
-                merged = jnp.where(lane128 == 31, last, first)
-                turned = pltpu.roll(merged, base + k, 1) if base + k else merged
-                acc_west = jnp.where(lane128 == base + k, turned, acc_west)
-                acc_east = jnp.where(lane128 == base + k + 31, turned, acc_east)
-        west_mask = jnp.broadcast_to(edge_mask[:, 0:1], (8, 128))
-        east_mask = jnp.broadcast_to(edge_mask[:, 31:32], (8, 128))
-        send_cols[rows, :] = acc_west * west_mask + pltpu.roll(acc_east, 1, 1) * east_mask
-
+    send_cols[0:ROWS, :] = ends[0] + pltpu.roll(ends[1], 1, 1)
 
     compact = jnp.zeros((8, 128), f32)
     for side in range(2):
@@ -341,7 +336,31 @@
         copy.start()
         heat_round.append(copy)
 
-    for copy in first_round + second_round:
+    level_inv[...] = jnp.zeros(level_inv.shape, f32)
+
+    @pl.loop(1, LEV)
+    def _(k):
+        level_inv[pl.ds(k, 1), :] = 1.0 / jnp.full((1, WIDE), h[k - 1] + h[k], f32)
+
+
+    weight = jnp.zeros((1, 128), f32)
+    lane_w = iota((1, 128), 1)
+    for k in range(LEV):
+        weight = jnp.where((lane_w & 15) == k, h[k], weight)
+    weight = weight * jnp.where((lane_w & 16) != 0, -0.5, 1.0)
+    level_weight = jnp.zeros((LEV, WIDE), f32)
+    level_row = iota((LEV, WIDE), 0)
+    for k in range(LEV):
+        level_weight = jnp.where(level_row == k, h[k], level_weight)
+    exists = (
+        jnp.where(gy < ny - 1, 1.0, 0.0).astype(f32),
+        jnp.where(gy > 0, 1.0, 0.0).astype(f32),
+    )
+
+    basis[0] = jnp.zeros((EXT, WIDE), f32)
+    weigh[...] = jnp.where(iota((ROWS, WIDE), 1) < COLS, 6.0 + damp_all, 0.0)
+
+    for copy in first_round:
         copy.wait()
 
     def beside(north, south):
@@ -363,24 +382,10 @@
     slope = jnp.where(is_east, 0.1, -0.1) * (other - own)
     through = 0.05 * speed * both - slope
     flux_lon[...] = through[0:ROWS, :]
-    weight = jnp.zeros((1, 128), f32)
-    lane_w = iota((1, 128), 1)
-    for k in range(LEV):
-        weight = jnp.where((lane_w & 15) == k, h[k], weight)
-    weight = weight * jnp.where((lane_w & 16) != 0, -0.5, 1.0)
     weighed = through * weight
     side_west = jnp.sum(jnp.where(lane_c < 32, weighed, 0.0), axis=1, keepdims=True)
     side_east = jnp.sum(
         jnp.where(is_east & (lane_c < 64), weighed, 0.0), axis=1, keepdims=True
-    )
-
-    level_weight = jnp.zeros((LEV, WIDE), f32)
-    level_row = iota((LEV, WIDE), 0)
-    for k in range(LEV):
-        level_weight = jnp.where(level_row == k, h[k], level_weight)
-    exists = (
-        jnp.where(gy < ny - 1, 1.0, 0.0).astype(f32),
-        jnp.where(gy > 0, 1.0, 0.0).astype(f32),
     )
 
     def side_flux(mine, theirs, speeds, sign):
@@ -443,7 +448,8 @@
     )
     inv = mask[...] * inverse(6.0 + damp_ext)
     scale[...] = 1.5 * inv
-    weigh[...] = jnp.where(iota((ROWS, WIDE), 1) < COLS, 6.0 + damp_all, 0.0)
+    for copy in second_round:
+        copy.wait()
     forcing = assemble(
         basis[1, 0:ROWS, :],
         lambda slot: recv_halo_rows[slot],
@@ -474,7 +480,6 @@
         ],
         axis=0,
     )
-    basis[0] = jnp.zeros((EXT, WIDE), f32)
     basis[1] = forcing * inv
 
     def folded(value):
@@ -673,6 +678,7 @@
         vmem(EXT, WIDE),
         vmem(24, WIDE),
         vmem(3, ROWS, WIDE),
+        vmem(2, ROWS, 128),
         vmem(2, 40, WIDE),
         vmem(2, LEV, WIDE),
         vmem(2, 40, WIDE),

time: 26.9 us -> 26.7 us (level)
  no operation moved by 1% of the time
where the time goes in v1:
time: 26.7 us; the launch traced here: 26.6 us
  Pallas kernels  25.9 us (97%)
  between operations  0.64 us (2%)
    pallas_call x1, Pallas kernels, body(): tracer, surface = call(*operands)  24.4 us
    pallas_call x1, Pallas kernels, body(): pl.pallas_call(store, out_shape=[jax.ShapeDtypeStruct((2, LEV, ROWS, COLS...  1.5 us

profile of v1, /device:TPU:1, one launch (start us, length us, event | category | flops | bytes accessed | tf_op | source)
XLA Modules:
  0.0 26.6 jit_solution(1673682330353403143)
XLA Ops:
  0.6 24.4 %shard_map.68 = (f32[2,16,48,288]{3,2,1,0:T(8,128)S(1)}, f32[48,288]{1,0:T(8,128)S(1)}) custom-call(f32[4,16,48,288]{3,2,1,0:T(8,128)} %ocean.1, f32[16]{0:T(128)} %thick.1, f32[48,288]{1,0:T(8,128)} %mixing.1, f32[48,288]{1,0:T(8,128)} %damping.1, s32[32,64]{1,0:T(8,128)} %blocks.1), custom_call_target="tpu_custom_call" | custom-call | tf_op jit(solution)/shard_map/pallas_call | solution.py:742
  25.1 1.5 %shard_map.69 = (f32[2,16,48,288]{3,2,1,0:T(8,128)}, f32[48,288]{1,0:T(8,128)}) custom-call(f32[2,16,48,288]{3,2,1,0:T(8,128)S(1)} %get-tuple-element.4.tracer, f32[48,288]{1,0:T(8,128)S(1)} %get-tuple-element.5.surface), custom_call_target="tpu_custom_call" | custom-call | tf_op jit(solution)/shard_map/pallas_call | solution.py:744

commit v2 on v1

--- a/solution.py
+++ b/solution.py
@@ -77,7 +77,9 @@
     flat,
     ends,
     send_rows,
+    send_strip,
     send_heat,
+    recv_strip,
     recv_rows,
     recv_heat,
     send_cols,
@@ -94,11 +96,10 @@
     basis,
     halo_rows,
     halo_cols,
-    halo_corner,
     recv_halo_rows,
     recv_halo_cols,
-    recv_halo_corner,
     message,
+    first_message,
     first_sum,
     second_message,
     second_sum,
@@ -165,11 +166,8 @@
     damp_low = padded(damp[0:8, :])
     damp_high = padded(damp[ROWS - 8 : ROWS, :])
     damp_rows = row_pack(damp_low, damp_high)
-    for side in range(2):
-        send_rows[side, 32:40, :] = damp_rows
     damp_all = padded(damp[...])
     send_cols[ROWS : 2 * ROWS, :] = column_pack(damp_all[:, 0:128], damp_all[:, 256:384])
-    send_corner[16:24, :] = column_pack(damp_rows[:, 0:128], damp_rows[:, 256:384])
 
     def remote(source, target, index, step, sends=send_sem, recvs=recv_sem):
         return pltpu.make_async_remote_copy(
@@ -257,7 +255,14 @@
         send_heat[side] = heat
         send_rows[side, 0:16, :] = heat - 0.5 * salt
         send_rows[side, 16:32, :] = padded(state[3, :, edge_row, :]) * edge_mask
-        first_round.append(remote(send_rows.at[side], recv_rows.at[side], side, step))
+        send_strip[side, 0:32, :] = send_rows[side, :, 0:128]
+        send_strip[side, 32:64, :] = send_rows[side, :, 128:256]
+        tail = jnp.zeros((8, 128), f32)
+        for part in range(4):
+            third = send_rows[side, 8 * part : 8 * part + 8, 256:384]
+            tail = jnp.where(lane128 // 32 == part, pltpu.roll(third, 32 * part, 1), tail)
+        send_strip[side, 64:72, :] = tail
+        first_round.append(remote(send_strip.at[side], recv_strip.at[side], side, step))
 
     pl.semaphore_wait(barrier, partners)
     for copy in first_round:
@@ -277,15 +282,12 @@
             compact = jnp.where(
                 inside & (lane128 % 16 >= 4) & (lane128 % 16 < 8), last, compact
             )
-    send_corner[0:8, :] = compact
     send_cols[2 * ROWS :, :] = compact
     send_corner[8:16, :] = row_pack(send_cols[0:8, :], send_cols[ROWS - 8 : ROWS, :])
 
     second_round = []
     for side, step in enumerate((EAST, WEST)):
         second_round.append(remote(send_cols, recv_cols.at[side], 2 + side, step))
-    for place, step in enumerate(DIAGONAL):
-        second_round.append(remote(send_corner, recv_corner.at[place], 4 + place, step))
     for side, step in enumerate((NORTH, SOUTH)):
         second_round.append(
             remote(send_corner.at[pl.ds(8, 8)], recv_side.at[side], 10 + side, step)
@@ -305,13 +307,22 @@
     start = jnp.where(lane_f < COLS, start, 0.0)
     basis[1, 0:ROWS, :] = start
     packed_rows = row_pack(start[0:8, :], start[ROWS - 8 : ROWS, :])
-    halo_rows[...] = packed_rows
+    halo_rows[0] = jnp.where(sub < 4, pltpu.roll(start[ROWS - 8 : ROWS, :], 4, 0), damp_high)
+    halo_rows[1] = jnp.where(sub < 4, damp_low, pltpu.roll(start[0:8, :], 4, 0))
     halo_cols[...] = column_pack(start[:, 0:128], start[:, 256:384])
-    halo_corner[...] = column_pack(packed_rows[:, 0:128], packed_rows[:, 256:384])
+    for base, packed in ((8, damp_rows), (24, packed_rows)):
+        first = pltpu.roll(packed[:, 0:128], base, 1)
+        last = packed[:, 256:384]
+        last = pltpu.roll(last, (base - 24) % 128, 1) if base != 24 else last
+        compact = jnp.where((lane128 >= base) & (lane128 < base + 4), first, compact)
+        compact = jnp.where((lane128 >= base + 4) & (lane128 < base + 8), last, compact)
+    send_corner[0:8, :] = compact
     second_round = []
     for side, step in enumerate((NORTH, SOUTH)):
         second_round.append(
-            remote(halo_rows, recv_halo_rows.at[side], side, step, halo_send_sem, halo_recv_sem)
+            remote(
+                halo_rows.at[side], recv_halo_rows.at[side], side, step, halo_send_sem, halo_recv_sem
+            )
         )
     for side, step in enumerate((EAST, WEST)):
         second_round.append(
@@ -320,8 +331,8 @@
     for place, step in enumerate(DIAGONAL):
         second_round.append(
             remote(
-                halo_corner,
-                recv_halo_corner.at[place],
+                send_corner,
+                recv_corner.at[place],
                 4 + place,
                 step,
                 halo_send_sem,
@@ -360,8 +371,15 @@
     basis[0] = jnp.zeros((EXT, WIDE), f32)
     weigh[...] = jnp.where(iota((ROWS, WIDE), 1) < COLS, 6.0 + damp_all, 0.0)
 
-    for copy in first_round:
+    for copy in first_round + second_round:
         copy.wait()
+    for slot in range(2):
+        recv_rows[slot, :, 0:128] = recv_strip[slot, 0:32, :]
+        recv_rows[slot, :, 128:256] = recv_strip[slot, 32:64, :]
+        for part in range(4):
+            tail = recv_strip[slot, 64:72, :]
+            tail = pltpu.roll(tail, 128 - 32 * part, 1) if part else tail
+            recv_rows[slot, 8 * part : 8 * part + 8, 256:384] = jnp.where(lane128 < 32, tail, 0.0)
 
     def beside(north, south):
         return jnp.where(iota((8, 128), 0) < 4, north, south)
@@ -425,36 +443,38 @@
         )
         side_lat[side] = jnp.concatenate([side_lat[side][:, 0:256], third], axis=1)
 
-    def assemble(center, rows_in, cols_in, corner_in):
-        lane8 = iota((8, 128), 1)
+    def assemble(center, north_south, cols_in, base):
         lane48 = iota((ROWS, 128), 1)
         third = jnp.where(
             lane48 < 32, center[:, 256:384], jnp.where(lane48 < 64, cols_in(1), cols_in(0))
         )
         upper = jnp.concatenate([center[:, 0:256], third], axis=1)
-        north_south = jnp.where(sub < 4, rows_in(1), rows_in(0))
-        north = jnp.where(lane8 < 64, corner_in(3), corner_in(2))
-        south = jnp.where(lane8 < 64, corner_in(1), corner_in(0))
-        corner = jnp.where(iota((8, 128), 0) < 4, north, south)
-        third = jnp.where(lane8 < 32, north_south[:, 256:384], corner)
+        low = pltpu.roll(corners, 32 - base, 1)
+        high = pltpu.roll(corners, 120 - base, 1)
+        third = jnp.where(
+            lane128 < 32, north_south[:, 256:384], jnp.where(lane128 < 64, low, high)
+        )
         lower = jnp.concatenate([north_south[:, 0:256], third], axis=1)
         return jnp.concatenate([upper, lower], axis=0)
 
+    is_low = (lane128 & 7) < 4
+    corners = beside(
+        jnp.where(is_low, recv_corner[3, 0:8, :], recv_corner[2, 0:8, :]),
+        jnp.where(is_low, recv_corner[1, 0:8, :], recv_corner[0, 0:8, :]),
+    )
     damp_ext = assemble(
         damp_all,
-        lambda slot: recv_rows[slot, 32:40, :],
+        jnp.where(sub < 4, recv_halo_rows[1], recv_halo_rows[0]),
         lambda slot: recv_cols[slot, ROWS : 2 * ROWS, :],
-        lambda place: recv_corner[place, 16:24, :],
+        8,
     )
     inv = mask[...] * inverse(6.0 + damp_ext)
     scale[...] = 1.5 * inv
-    for copy in second_round:
-        copy.wait()
     forcing = assemble(
         basis[1, 0:ROWS, :],
-        lambda slot: recv_halo_rows[slot],
+        pltpu.roll(jnp.where(sub < 4, recv_halo_rows[0], recv_halo_rows[1]), 4, 0),
         lambda slot: recv_halo_cols[slot],
-        lambda place: recv_halo_corner[place],
+        24,
     )
     forcing = jnp.concatenate(
         [
@@ -528,7 +548,12 @@
         done.wait_send()
         return jnp.sum(target[...], axis=0)
 
-    spread(message, first_sum, nx, lambda d: (d, 0), gx, 0)
+    parts = message[...]
+    for shift in (64, 32, 16):
+        parts = parts + pltpu.roll(parts, shift, 1)
+    mine = lane128 // 16 == iota((8, 128), 0)
+    first_message[...] = jnp.sum(jnp.where(mine, parts, 0.0), axis=0, keepdims=True)
+    spread(first_message, first_sum, nx, lambda d: (d, 0), gx, 0)
 
     for copy in heat_round:
         copy.wait()
@@ -614,6 +639,7 @@
     lax.fori_loop(2, TILES, mix_tile, 0)
     sums = gathered(second_sum, ny, 1)
 
+    sums = jnp.where(mine, jnp.broadcast_to(sums, (8, 128)), 0.0)
     sums = jnp.broadcast_to(jnp.sum(sums, axis=1, keepdims=True), (8, 128))
     dots = [sums[i : i + 1, :] for i in range(8)]
     moment = dots[0:2] + [2.0 * dots[i] - dots[i % 2] for i in range(2, 8)]
@@ -679,14 +705,16 @@
         vmem(24, WIDE),
         vmem(3, ROWS, WIDE),
         vmem(2, ROWS, 128),
-        vmem(2, 40, WIDE),
+        vmem(2, 32, WIDE),
+        vmem(2, 72, 128),
         vmem(2, LEV, WIDE),
-        vmem(2, 40, WIDE),
+        vmem(2, 72, 128),
+        vmem(2, 32, WIDE),
         vmem(2, LEV, WIDE),
         vmem(2 * ROWS + 8, 128),
         vmem(2, 2 * ROWS + 8, 128),
-        vmem(24, 128),
-        vmem(4, 24, 128),
+        vmem(16, 128),
+        vmem(4, 16, 128),
         vmem(2, 8, 128),
         vmem(ROWS, 128),
         vmem(2 * LEV, WIDE),
@@ -695,16 +723,15 @@
         vmem(EXT, WIDE),
         vmem(ROWS, WIDE),
         vmem(6, EXT, WIDE),
-        vmem(8, WIDE),
+        vmem(2, 8, WIDE),
         vmem(ROWS, 128),
-        vmem(8, 128),
         vmem(2, 8, WIDE),
         vmem(2, ROWS, 128),
-        vmem(4, 8, 128),
         vmem(8, 128),
-        vmem(nx, 8, 128),
-        vmem(8, 128),
-        vmem(ny, 8, 128),
+        vmem(1, 128),
+        vmem(nx, 1, 128),
+        vmem(1, 128),
+        vmem(ny, 1, 128),
         dma((4,)),
         dma((4,)),
         dma((12,)),

time: 26.7 us -> 25.8 us (0.966)
  Pallas kernels: 25.9 us -> 25 us
    pallas_call x1, Pallas kernels: 24.4 us -> 23.5 us  [body(): tracer, surface = call(*operands)]
where the time goes in v2:
time: 25.8 us; the launch traced here: 25.7 us
  Pallas kernels  25 us (97%)
  between operations  0.64 us (2%)
    pallas_call x1, Pallas kernels, body(): tracer, surface = call(*operands)  23.5 us
    pallas_call x1, Pallas kernels, body(): pl.pallas_call(store, out_shape=[jax.ShapeDtypeStruct((2, LEV, ROWS, COLS...  1.5 us

profile of v2, /device:TPU:1, one launch (start us, length us, event | category | flops | bytes accessed | tf_op | source)
XLA Modules:
  0.0 25.7 jit_solution(2214463048209319370)
XLA Ops:
  0.6 23.5 %shard_map.68 = (f32[2,16,48,288]{3,2,1,0:T(8,128)S(1)}, f32[48,288]{1,0:T(8,128)S(1)}) custom-call(f32[4,16,48,288]{3,2,1,0:T(8,128)} %ocean.1, f32[16]{0:T(128)} %thick.1, f32[48,288]{1,0:T(8,128)} %mixing.1, f32[48,288]{1,0:T(8,128)} %damping.1, s32[32,64]{1,0:T(8,128)} %blocks.1), custom_call_target="tpu_custom_call" | custom-call | tf_op jit(solution)/shard_map/pallas_call | solution.py:769
  24.2 1.5 %shard_map.69 = (f32[2,16,48,288]{3,2,1,0:T(8,128)}, f32[48,288]{1,0:T(8,128)}) custom-call(f32[2,16,48,288]{3,2,1,0:T(8,128)S(1)} %get-tuple-element.4.tracer, f32[48,288]{1,0:T(8,128)S(1)} %get-tuple-element.5.surface), custom_call_target="tpu_custom_call" | custom-call | tf_op jit(solution)/shard_map/pallas_call | solution.py:771

commit v3 on v2

--- a/solution.py
+++ b/solution.py
@@ -98,7 +98,6 @@
     halo_cols,
     recv_halo_rows,
     recv_halo_cols,
-    message,
     first_message,
     first_sum,
     second_message,
@@ -318,16 +317,6 @@
         compact = jnp.where((lane128 >= base + 4) & (lane128 < base + 8), last, compact)
     send_corner[0:8, :] = compact
     second_round = []
-    for side, step in enumerate((NORTH, SOUTH)):
-        second_round.append(
-            remote(
-                halo_rows.at[side], recv_halo_rows.at[side], side, step, halo_send_sem, halo_recv_sem
-            )
-        )
-    for side, step in enumerate((EAST, WEST)):
-        second_round.append(
-            remote(halo_cols, recv_halo_cols.at[side], 2 + side, step, halo_send_sem, halo_recv_sem)
-        )
     for place, step in enumerate(DIAGONAL):
         second_round.append(
             remote(
@@ -338,6 +327,16 @@
                 halo_send_sem,
                 halo_recv_sem,
             )
+        )
+    for side, step in enumerate((NORTH, SOUTH)):
+        second_round.append(
+            remote(
+                halo_rows.at[side], recv_halo_rows.at[side], side, step, halo_send_sem, halo_recv_sem
+            )
+        )
+    for side, step in enumerate((EAST, WEST)):
+        second_round.append(
+            remote(halo_cols, recv_halo_cols.at[side], 2 + side, step, halo_send_sem, halo_recv_sem)
         )
     for copy in second_round:
         copy.start()
@@ -368,10 +367,9 @@
         jnp.where(gy > 0, 1.0, 0.0).astype(f32),
     )
 
-    basis[0] = jnp.zeros((EXT, WIDE), f32)
     weigh[...] = jnp.where(iota((ROWS, WIDE), 1) < COLS, 6.0 + damp_all, 0.0)
 
-    for copy in first_round + second_round:
+    for copy in first_round:
         copy.wait()
     for slot in range(2):
         recv_rows[slot, :, 0:128] = recv_strip[slot, 0:32, :]
@@ -380,6 +378,23 @@
             tail = recv_strip[slot, 64:72, :]
             tail = pltpu.roll(tail, 128 - 32 * part, 1) if part else tail
             recv_rows[slot, 8 * part : 8 * part + 8, 256:384] = jnp.where(lane128 < 32, tail, 0.0)
+
+    def side_flux(mine, theirs, speeds, sign):
+        return speeds * (mine + theirs) - (0.1 * sign) * (theirs - mine)
+
+    side_lat = []
+    speed_lat = []
+    for side, sign in ((0, 1.0), (1, -1.0)):
+        slot = 1 - side
+        s_mine = send_rows[side, 0:16, :]
+        s_theirs = recv_rows[slot, 0:16, :] * exists[side]
+        speeds = 0.05 * (send_rows[side, 16:32, :] + recv_rows[slot, 16:32, :] * exists[side])
+        speed_lat.append(speeds)
+        flux = side_flux(s_mine, s_theirs, speeds, sign)
+        side_lat.append(jnp.sum(flux * level_weight, axis=0, keepdims=True))
+
+    for copy in second_round:
+        copy.wait()
 
     def beside(north, south):
         return jnp.where(iota((8, 128), 0) < 4, north, south)
@@ -406,20 +421,6 @@
         jnp.where(is_east & (lane_c < 64), weighed, 0.0), axis=1, keepdims=True
     )
 
-    def side_flux(mine, theirs, speeds, sign):
-        return speeds * (mine + theirs) - (0.1 * sign) * (theirs - mine)
-
-    side_lat = []
-    speed_lat = []
-    for side, sign in ((0, 1.0), (1, -1.0)):
-        slot = 1 - side
-        s_mine = send_rows[side, 0:16, :]
-        s_theirs = recv_rows[slot, 0:16, :] * exists[side]
-        speeds = 0.05 * (send_rows[side, 16:32, :] + recv_rows[slot, 16:32, :] * exists[side])
-        speed_lat.append(speeds)
-        flux = side_flux(s_mine, s_theirs, speeds, sign)
-        side_lat.append(jnp.sum(flux * level_weight, axis=0, keepdims=True))
-
     is_first = (lane128 & 15) < 4
     is_north = lane128 < 64
     mine = jnp.where(is_first, recv_cols[1, 2 * ROWS :, :], recv_cols[0, 2 * ROWS :, :])
@@ -503,28 +504,42 @@
     basis[1] = forcing * inv
 
     def folded(value):
-        value = value[:, 0:128] + value[:, 128:256] + value[:, 256:384]
-        return jnp.sum(value, axis=0, keepdims=True)
-
-    @pl.loop(0, 4)
-    def _(index):
+        rows = [value[8 * i : 8 * i + 8, :] for i in range(TILES)]
+        value = (rows[0] + rows[1]) + (rows[2] + rows[3]) + (rows[4] + rows[5])
+        return value[:, 0:128] + value[:, 128:256] + value[:, 256:384]
+
+    parts = []
+    for index in range(4):
         q = basis[index + 1]
         pair = east_of(q) + west_of(q)
         column = q + 0.5 * pair
         around = pair + pltpu.roll(column, EXT - 1, 0) + pltpu.roll(column, 1, 0)
         image = scale[...] * around - 0.5 * q
-        later = jnp.where(index == 0, 0.0, 1.0)
-        after = image + later * (image - basis[index])
-        basis[index + 2] = after
+        after = image if index == 0 else 2.0 * image - basis[index]
+        if index < 3:
+            basis[index + 2] = after
         weighed = weigh[...] * q[0:ROWS, :]
-        message[pl.ds(2 * index, 1), :] = folded(weighed * q[0:ROWS, :])
-        message[pl.ds(2 * index + 1, 1), :] = folded(weighed * after[0:ROWS, :])
+        parts.append(folded(weighed * q[0:ROWS, :]))
+        parts.append(folded(weighed * after[0:ROWS, :]))
+
+    for width in (64, 32, 16):
+        half = len(parts) // 2
+        parts = [
+            jnp.where(
+                (lane128 & width) == 0,
+                low + pltpu.roll(low, 128 - width, 1),
+                high + pltpu.roll(high, width, 1),
+            )
+            for low, high in zip(parts[:half], parts[half:])
+        ]
+    first_message[...] = jnp.sum(parts[0], axis=0, keepdims=True)
 
     def spread(source, target, count, along, mine, base):
         target[mine] = source[...]
 
         @pl.loop(1, count)
-        def _(d):
+        def _(turn):
+            d = count // 2 + jnp.where(turn % 2 == 0, -(turn // 2), turn // 2)
             pltpu.make_async_remote_copy(
                 src_ref=source,
                 dst_ref=target.at[mine],
@@ -548,11 +563,6 @@
         done.wait_send()
         return jnp.sum(target[...], axis=0)
 
-    parts = message[...]
-    for shift in (64, 32, 16):
-        parts = parts + pltpu.roll(parts, shift, 1)
-    mine = lane128 // 16 == iota((8, 128), 0)
-    first_message[...] = jnp.sum(jnp.where(mine, parts, 0.0), axis=0, keepdims=True)
     spread(first_message, first_sum, nx, lambda d: (d, 0), gx, 0)
 
     for copy in heat_round:
@@ -639,7 +649,8 @@
     lax.fori_loop(2, TILES, mix_tile, 0)
     sums = gathered(second_sum, ny, 1)
 
-    sums = jnp.where(mine, jnp.broadcast_to(sums, (8, 128)), 0.0)
+    own_lanes = lane128 // 16 == iota((8, 128), 0)
+    sums = jnp.where(own_lanes, jnp.broadcast_to(sums, (8, 128)), 0.0)
     sums = jnp.broadcast_to(jnp.sum(sums, axis=1, keepdims=True), (8, 128))
     dots = [sums[i : i + 1, :] for i in range(8)]
     moment = dots[0:2] + [2.0 * dots[i] - dots[i % 2] for i in range(2, 8)]
@@ -727,7 +738,6 @@
         vmem(ROWS, 128),
         vmem(2, 8, WIDE),
         vmem(2, ROWS, 128),
-        vmem(8, 128),
         vmem(1, 128),
         vmem(nx, 1, 128),
         vmem(1, 128),

time: 25.8 us -> 25.8 us (level)
  no operation moved by 1% of the time
where the time goes in v3:
time: 25.8 us; the launch traced here: 25.6 us
  Pallas kernels  25 us (97%)
  between operations  0.64 us (2%)
    pallas_call x1, Pallas kernels, body(): tracer, surface = call(*operands)  23.5 us
    pallas_call x1, Pallas kernels, body(): pl.pallas_call(store, out_shape=[jax.ShapeDtypeStruct((2, LEV, ROWS, COLS...  1.5 us

profile of v3, /device:TPU:1, one launch (start us, length us, event | category | flops | bytes accessed | tf_op | source)
XLA Modules:
  0.0 25.6 jit_solution(5651434106945350206)
XLA Ops:
  0.6 23.5 %shard_map.68 = (f32[2,16,48,288]{3,2,1,0:T(8,128)S(1)}, f32[48,288]{1,0:T(8,128)S(1)}) custom-call(f32[4,16,48,288]{3,2,1,0:T(8,128)} %ocean.1, f32[16]{0:T(128)} %thick.1, f32[48,288]{1,0:T(8,128)} %mixing.1, f32[48,288]{1,0:T(8,128)} %damping.1, s32[32,64]{1,0:T(8,128)} %blocks.1), custom_call_target="tpu_custom_call" | custom-call | tf_op jit(solution)/shard_map/pallas_call | solution.py:779
  24.1 1.5 %shard_map.69 = (f32[2,16,48,288]{3,2,1,0:T(8,128)}, f32[48,288]{1,0:T(8,128)}) custom-call(f32[2,16,48,288]{3,2,1,0:T(8,128)S(1)} %get-tuple-element.4.tracer, f32[48,288]{1,0:T(8,128)S(1)} %get-tuple-element.5.surface), custom_call_target="tpu_custom_call" | custom-call | tf_op jit(solution)/shard_map/pallas_call | solution.py:781

commit v4 on v3

--- a/solution.py
+++ b/solution.py
@@ -91,6 +91,8 @@
     flux_north,
     flux_prev,
     ratio,
+    carried,
+    taken,
     scale,
     weigh,
     basis,
@@ -369,6 +371,26 @@
 
     weigh[...] = jnp.where(iota((ROWS, WIDE), 1) < COLS, 6.0 + damp_all, 0.0)
 
+    small[3].wait()
+
+    @pl.loop(0, 2)
+    def _(part):
+        rows = pl.ds(pl.multiple_of(ROWS // 2 * part, 8), ROWS // 2)
+        coefficient = padded(mix[rows, :])
+        here = mask[rows, :]
+
+        def level(k, ratio_low):
+            below = coefficient * level_inv[pl.ds(k, 1), :]
+            above = coefficient * level_inv[pl.ds(k + 1, 1), :]
+            pivot = inverse(h[k] + above + below * (1.0 - ratio_low))
+            ratio_now = above * pivot
+            ratio[k, rows, :] = ratio_now
+            carried[k, rows, :] = below * pivot
+            taken[k, rows, :] = h[k] * pivot * here
+            return ratio_now
+
+        lax.fori_loop(0, LEV, level, jnp.zeros((ROWS // 2, WIDE), f32), unroll=4)
+
     for copy in first_round:
         copy.wait()
     for slot in range(2):
@@ -576,8 +598,6 @@
         salt_theirs = 2.0 * (heat_theirs - recv_rows[slot, 0:16, :] * exists[side])
         target[0:16, :] = side_flux(heat_mine, heat_theirs, speed_lat[side], sign)
         target[16:32, :] = side_flux(salt_mine, salt_theirs, speed_lat[side], sign)
-    small[3].wait()
-
     edge_lane = (lane128 == 31) | (lane128 == 127)
 
     def mix_tile(i, _):
@@ -585,12 +605,11 @@
         row = pl.ds(next_row(i), 1)
         here = mask[rows, :]
         beyond = mask[row, :]
-        coefficient = padded(mix[rows, :])
         through = flux_lon[rows, :]
         use_north = (sub == 7) & (i == TILES - 1)
 
         def level(k, carry):
-            ratio_low, heat_low, salt_low = carry
+            heat_low, salt_low = carry
             u = padded(state[2, k, rows, :]) * here
             v = padded(state[3, k, rows, :]) * here
             v_row = padded(state[3, k, row, :]) * beyond
@@ -599,11 +618,6 @@
             v_pair = 0.05 * (v + v_north)
             lon_far, lon_near = u_pair - 0.1, u_pair + 0.1
             lat_far, lat_near = v_pair - 0.1, v_pair + 0.1
-            below = coefficient * level_inv[pl.ds(k, 1), :]
-            above = coefficient * level_inv[pl.ds(k + 1, 1), :]
-            pivot = inverse(h[k] + above + below * (1.0 - ratio_low))
-            ratio_now = above * pivot
-            ratio[k] = ratio_now
             found = []
             for tracer, low in ((0, heat_low), (1, salt_low)):
                 plane = tracer * LEV + k
@@ -621,19 +635,19 @@
                     sub == 0, flux_prev[pl.ds(plane, 1), :], pltpu.roll(lat, 1, 0)
                 )
                 flux_prev[pl.ds(plane, 1), :] = lat[7:8, :]
-                advected = here * (c - (lon - west_of(lon)) - (lat - lat_south))
-                value = (h[k] * advected + below * low) * pivot
+                advected = c - (lon - west_of(lon)) - (lat - lat_south)
+                value = taken[k, rows, :] * advected + carried[k, rows, :] * low
                 tracer_out[tracer, k, rows, :] = value[:, 0:COLS]
                 found.append(value)
-            return ratio_now, found[0], found[1]
+            return found[0], found[1]
 
         zero = jnp.zeros((8, WIDE), f32)
-        _, heat, salt = lax.fori_loop(0, LEV, level, (zero, zero, zero), unroll=4)
+        heat, salt = lax.fori_loop(0, LEV, level, (zero, zero), unroll=4)
 
         def back(step, carry):
             k = LEV - 2 - step
             heat_up, salt_up = carry
-            share = ratio[k][:, 0:COLS]
+            share = ratio[k, rows, 0:COLS]
             heat_up = tracer_out[0, k, rows, :] + share * heat_up
             salt_up = tracer_out[1, k, rows, :] + share * salt_up
             tracer_out[0, k, rows, :] = heat_up
@@ -730,7 +744,9 @@
         vmem(ROWS, 128),
         vmem(2 * LEV, WIDE),
         vmem(2 * LEV, WIDE),
-        vmem(LEV, 8, WIDE),
+        vmem(LEV, ROWS, WIDE),
+        vmem(LEV, ROWS, WIDE),
+        vmem(LEV, ROWS, WIDE),
         vmem(EXT, WIDE),
         vmem(ROWS, WIDE),
         vmem(6, EXT, WIDE),

time: 25.8 us -> 25.9 us (level)
  no operation moved by 1% of the time
where the time goes in v4:
time: 25.9 us; the launch traced here: 25.7 us
  Pallas kernels  25.1 us (97%)
  between operations  0.64 us (2%)
    pallas_call x1, Pallas kernels, body(): tracer, surface = call(*operands)  23.6 us
    pallas_call x1, Pallas kernels, body(): pl.pallas_call(store, out_shape=[jax.ShapeDtypeStruct((2, LEV, ROWS, COLS...  1.5 us

profile of v4, /device:TPU:1, one launch (start us, length us, event | category | flops | bytes accessed | tf_op | source)
XLA Modules:
  0.0 25.7 jit_solution(11993209276153626391)
XLA Ops:
  0.6 23.6 %shard_map.68 = (f32[2,16,48,288]{3,2,1,0:T(8,128)S(1)}, f32[48,288]{1,0:T(8,128)S(1)}) custom-call(f32[4,16,48,288]{3,2,1,0:T(8,128)} %ocean.1, f32[16]{0:T(128)} %thick.1, f32[48,288]{1,0:T(8,128)} %mixing.1, f32[48,288]{1,0:T(8,128)} %damping.1, s32[32,64]{1,0:T(8,128)} %blocks.1), custom_call_target="tpu_custom_call" | custom-call | tf_op jit(solution)/shard_map/pallas_call | solution.py:795
  24.2 1.5 %shard_map.69 = (f32[2,16,48,288]{3,2,1,0:T(8,128)}, f32[48,288]{1,0:T(8,128)}) custom-call(f32[2,16,48,288]{3,2,1,0:T(8,128)S(1)} %get-tuple-element.4.tracer, f32[48,288]{1,0:T(8,128)S(1)} %get-tuple-element.5.surface), custom_call_target="tpu_custom_call" | custom-call | tf_op jit(solution)/shard_map/pallas_call | solution.py:797

commit v5 on v4

--- a/solution.py
+++ b/solution.py
@@ -132,11 +132,18 @@
 
     def load(index):
         levels = pl.ds(group * index, group)
+        rows = pl.ds(8, ROWS - 16)
         return pltpu.make_async_copy(
-            ocean.at[:, levels, :, :], state.at[:, levels, :, :], load_sem.at[index]
-        )
-
-    for copy in small[:3] + [load(index) for index in range(4)] + small[3:]:
+            ocean.at[:, levels, rows, :], state.at[:, levels, rows, :], load_sem.at[index]
+        )
+
+    edge_loads = [
+        pltpu.make_async_copy(
+            ocean.at[:, :, rows, :], state.at[:, :, rows, :], load_sem.at[4 + index]
+        )
+        for index, rows in enumerate((pl.ds(0, 8), pl.ds(ROWS - 8, 8)))
+    ]
+    for copy in small[:3] + edge_loads + [load(index) for index in range(4)] + small[3:]:
         copy.start()
 
     barrier = pltpu.get_barrier_semaphore()
@@ -215,8 +222,40 @@
             jnp.where(sub == 7, turned[(i + 1) % TILES], turned[i]) for i in range(TILES)
         ]
 
+    def strips():
+        return [
+            remote(send_strip.at[side], recv_strip.at[side], side, step)
+            for side, step in enumerate((NORTH, SOUTH))
+        ]
+
+    def send_edge_rows():
+        for side, (edge_row, step) in enumerate(((ROWS - 1, NORTH), (0, SOUTH))):
+            edge_mask = mask[edge_row : edge_row + 1, :]
+            heat = padded(state[0, :, edge_row, :]) * edge_mask
+            salt = padded(state[1, :, edge_row, :]) * edge_mask
+            send_heat[side] = heat
+            send_rows[side, 0:16, :] = heat - 0.5 * salt
+            send_rows[side, 16:32, :] = padded(state[3, :, edge_row, :]) * edge_mask
+            send_strip[side, 0:32, :] = send_rows[side, :, 0:128]
+            send_strip[side, 32:64, :] = send_rows[side, :, 128:256]
+            tail = jnp.zeros((8, 128), f32)
+            for part in range(4):
+                third = send_rows[side, 8 * part : 8 * part + 8, 256:384]
+                tail = jnp.where(lane128 // 32 == part, pltpu.roll(third, 32 * part, 1), tail)
+            send_strip[side, 64:72, :] = tail
+        pl.semaphore_wait(barrier, partners)
+        for copy in strips():
+            copy.start()
+
+    for copy in edge_loads:
+        copy.wait()
+
     @pl.loop(0, LEV // 2)
     def _(pair):
+        @pl.when(pair == LEV // 4)
+        def _():
+            send_edge_rows()
+
         @pl.when(lax.rem(pair, group // 2) == 0)
         def _():
             load(pair // (group // 2)).wait()
@@ -248,27 +287,6 @@
                 flat[part, rows, :] += sums[i][part]
         pack_ends(pair)
 
-    first_round = []
-    for side, (edge_row, step) in enumerate(((ROWS - 1, NORTH), (0, SOUTH))):
-        edge_mask = mask[edge_row : edge_row + 1, :]
-        heat = padded(state[0, :, edge_row, :]) * edge_mask
-        salt = padded(state[1, :, edge_row, :]) * edge_mask
-        send_heat[side] = heat
-        send_rows[side, 0:16, :] = heat - 0.5 * salt
-        send_rows[side, 16:32, :] = padded(state[3, :, edge_row, :]) * edge_mask
-        send_strip[side, 0:32, :] = send_rows[side, :, 0:128]
-        send_strip[side, 32:64, :] = send_rows[side, :, 128:256]
-        tail = jnp.zeros((8, 128), f32)
-        for part in range(4):
-            third = send_rows[side, 8 * part : 8 * part + 8, 256:384]
-            tail = jnp.where(lane128 // 32 == part, pltpu.roll(third, 32 * part, 1), tail)
-        send_strip[side, 64:72, :] = tail
-        first_round.append(remote(send_strip.at[side], recv_strip.at[side], side, step))
-
-    pl.semaphore_wait(barrier, partners)
-    for copy in first_round:
-        copy.start()
-
     send_cols[0:ROWS, :] = ends[0] + pltpu.roll(ends[1], 1, 1)
 
     compact = jnp.zeros((8, 128), f32)
@@ -295,7 +313,7 @@
         )
     for copy in second_round:
         copy.start()
-    first_round = first_round + second_round
+    first_round = strips() + second_round
 
     lane_f = iota((ROWS, WIDE), 1)
     row_f = iota((ROWS, WIDE), 0)
@@ -758,7 +776,7 @@
         vmem(nx, 1, 128),
         vmem(1, 128),
         vmem(ny, 1, 128),
-        dma((4,)),
+        dma((6,)),
         dma((4,)),
         dma((12,)),
         dma((12,)),

time: 25.9 us -> 26 us (level)
  no operation moved by 1% of the time
where the time goes in v5:
time: 26 us; the launch traced here: 25.7 us
  Pallas kernels  25.1 us (97%)
  between operations  0.64 us (2%)
    pallas_call x1, Pallas kernels, body(): tracer, surface = call(*operands)  23.6 us
    pallas_call x1, Pallas kernels, body(): pl.pallas_call(store, out_shape=[jax.ShapeDtypeStruct((2, LEV, ROWS, COLS...  1.5 us

profile of v5, /device:TPU:1, one launch (start us, length us, event | category | flops | bytes accessed | tf_op | source)
XLA Modules:
  0.0 25.7 jit_solution(9295618792401277041)
XLA Ops:
  0.6 23.6 %shard_map.68 = (f32[2,16,48,288]{3,2,1,0:T(8,128)S(1)}, f32[48,288]{1,0:T(8,128)S(1)}) custom-call(f32[4,16,48,288]{3,2,1,0:T(8,128)} %ocean.1, f32[16]{0:T(128)} %thick.1, f32[48,288]{1,0:T(8,128)} %mixing.1, f32[48,288]{1,0:T(8,128)} %damping.1, s32[32,64]{1,0:T(8,128)} %blocks.1), custom_call_target="tpu_custom_call" | custom-call | tf_op jit(solution)/shard_map/pallas_call | solution.py:813
  24.2 1.5 %shard_map.69 = (f32[2,16,48,288]{3,2,1,0:T(8,128)}, f32[48,288]{1,0:T(8,128)}) custom-call(f32[2,16,48,288]{3,2,1,0:T(8,128)S(1)} %get-tuple-element.4.tracer, f32[48,288]{1,0:T(8,128)S(1)} %get-tuple-element.5.surface), custom_call_target="tpu_custom_call" | custom-call | tf_op jit(solution)/shard_map/pallas_call | solution.py:815

commit v6 on v4

--- a/solution.py
+++ b/solution.py
@@ -128,7 +128,7 @@
         pltpu.make_async_copy(damping, damp, small_sem.at[2]),
         pltpu.make_async_copy(mixing, mix, small_sem.at[3]),
     ]
-    group = LEV // 4
+    group = LEV // 8
 
     def load(index):
         levels = pl.ds(group * index, group)
@@ -136,7 +136,7 @@
             ocean.at[:, levels, :, :], state.at[:, levels, :, :], load_sem.at[index]
         )
 
-    for copy in small[:3] + [load(index) for index in range(4)] + small[3:]:
+    for copy in small[:3] + [load(index) for index in range(8)] + small[3:]:
         copy.start()
 
     barrier = pltpu.get_barrier_semaphore()
@@ -758,7 +758,7 @@
         vmem(nx, 1, 128),
         vmem(1, 128),
         vmem(ny, 1, 128),
-        dma((4,)),
+        dma((8,)),
         dma((4,)),
         dma((12,)),
         dma((12,)),

time: 25.9 us -> 26.2 us (1.012)
  Pallas kernels: 25.1 us -> 25.4 us
    pallas_call x1, Pallas kernels: 23.6 us -> 23.9 us  [body(): tracer, surface = call(*operands)]
where the time goes in v6:
time: 26.2 us; the launch traced here: 26.1 us
  Pallas kernels  25.4 us (97%)
  between operations  0.64 us (2%)
    pallas_call x1, Pallas kernels, body(): tracer, surface = call(*operands)  23.9 us
    pallas_call x1, Pallas kernels, body(): pl.pallas_call(store, out_shape=[jax.ShapeDtypeStruct((2, LEV, ROWS, COLS...  1.5 us

profile of v6, /device:TPU:1, one launch (start us, length us, event | category | flops | bytes accessed | tf_op | source)
XLA Modules:
  0.0 26.1 jit_solution(17860820992864131396)
XLA Ops:
  0.6 23.9 %shard_map.68 = (f32[2,16,48,288]{3,2,1,0:T(8,128)S(1)}, f32[48,288]{1,0:T(8,128)S(1)}) custom-call(f32[4,16,48,288]{3,2,1,0:T(8,128)} %ocean.1, f32[16]{0:T(128)} %thick.1, f32[48,288]{1,0:T(8,128)} %mixing.1, f32[48,288]{1,0:T(8,128)} %damping.1, s32[32,64]{1,0:T(8,128)} %blocks.1), custom_call_target="tpu_custom_call" | custom-call | tf_op jit(solution)/shard_map/pallas_call | solution.py:795
  24.6 1.5 %shard_map.69 = (f32[2,16,48,288]{3,2,1,0:T(8,128)}, f32[48,288]{1,0:T(8,128)}) custom-call(f32[2,16,48,288]{3,2,1,0:T(8,128)S(1)} %get-tuple-element.4.tracer, f32[48,288]{1,0:T(8,128)S(1)} %get-tuple-element.5.surface), custom_call_target="tpu_custom_call" | custom-call | tf_op jit(solution)/shard_map/pallas_call | solution.py:797

commit v7 on v4

--- a/solution.py
+++ b/solution.py
@@ -657,10 +657,10 @@
         lax.fori_loop(0, LEV - 1, back, (heat[:, 0:COLS], salt[:, 0:COLS]), unroll=5)
         return 0
 
-    lax.fori_loop(0, 2, mix_tile, 0)
+    lax.fori_loop(0, 1, mix_tile, 0)
     second_message[...] = gathered(first_sum, nx, 0)
     spread(second_message, second_sum, ny, lambda d: (0, d), gy, 1)
-    lax.fori_loop(2, TILES, mix_tile, 0)
+    lax.fori_loop(1, TILES, mix_tile, 0)
     sums = gathered(second_sum, ny, 1)
 
     own_lanes = lane128 // 16 == iota((8, 128), 0)

time: 25.9 us -> 26.9 us (1.039)
  Pallas kernels: 25.1 us -> 26.1 us
    pallas_call x1, Pallas kernels: 23.6 us -> 24.6 us  [body(): tracer, surface = call(*operands)]
where the time goes in v7:
time: 26.9 us; the launch traced here: 26.7 us
  Pallas kernels  26.1 us (97%)
  between operations  0.64 us (2%)
    pallas_call x1, Pallas kernels, body(): tracer, surface = call(*operands)  24.6 us
    pallas_call x1, Pallas kernels, body(): pl.pallas_call(store, out_shape=[jax.ShapeDtypeStruct((2, LEV, ROWS, COLS...  1.5 us

profile of v7, /device:TPU:1, one launch (start us, length us, event | category | flops | bytes accessed | tf_op | source)
XLA Modules:
  0.0 26.7 jit_solution(9947453504136073611)
XLA Ops:
  0.6 24.6 %shard_map.68 = (f32[2,16,48,288]{3,2,1,0:T(8,128)S(1)}, f32[48,288]{1,0:T(8,128)S(1)}) custom-call(f32[4,16,48,288]{3,2,1,0:T(8,128)} %ocean.1, f32[16]{0:T(128)} %thick.1, f32[48,288]{1,0:T(8,128)} %mixing.1, f32[48,288]{1,0:T(8,128)} %damping.1, s32[32,64]{1,0:T(8,128)} %blocks.1), custom_call_target="tpu_custom_call" | custom-call | tf_op jit(solution)/shard_map/pallas_call | solution.py:795
  25.2 1.5 %shard_map.69 = (f32[2,16,48,288]{3,2,1,0:T(8,128)}, f32[48,288]{1,0:T(8,128)}) custom-call(f32[2,16,48,288]{3,2,1,0:T(8,128)S(1)} %get-tuple-element.4.tracer, f32[48,288]{1,0:T(8,128)S(1)} %get-tuple-element.5.surface), custom_call_target="tpu_custom_call" | custom-call | tf_op jit(solution)/shard_map/pallas_call | solution.py:797

commit v8 on v4

--- a/solution.py
+++ b/solution.py
@@ -142,8 +142,11 @@
     barrier = pltpu.get_barrier_semaphore()
     for step in DIAGONAL:
         greet(step)
-    pl.loop(1, nx)(lambda d: greet((d, 0)))
-    pl.loop(1, ny)(lambda d: greet((0, d)))
+    def nearest(turn, count):
+        return jnp.where(turn % 2 == 1, (turn + 1) // 2, count - turn // 2)
+
+    pl.loop(1, ny)(lambda turn: greet((0, nearest(turn, ny))))
+    pl.loop(1, nx)(lambda turn: greet((nearest(turn, nx), 0)))
     partners = len(DIAGONAL) + nx - 1 + ny - 1
 
     block_rows, block_cols = blk.shape

time: 25.9 us -> 25.9 us (level)
  no operation moved by 1% of the time
where the time goes in v8:
time: 25.9 us; the launch traced here: 25.7 us
  Pallas kernels  25.1 us (97%)
  between operations  0.64 us (2%)
    pallas_call x1, Pallas kernels, body(): tracer, surface = call(*operands)  23.6 us
    pallas_call x1, Pallas kernels, body(): pl.pallas_call(store, out_shape=[jax.ShapeDtypeStruct((2, LEV, ROWS, COLS...  1.5 us

profile of v8, /device:TPU:1, one launch (start us, length us, event | category | flops | bytes accessed | tf_op | source)
XLA Modules:
  0.0 25.7 jit_solution(5901329991026067419)
XLA Ops:
  0.6 23.6 %shard_map.68 = (f32[2,16,48,288]{3,2,1,0:T(8,128)S(1)}, f32[48,288]{1,0:T(8,128)S(1)}) custom-call(f32[4,16,48,288]{3,2,1,0:T(8,128)} %ocean.1, f32[16]{0:T(128)} %thick.1, f32[48,288]{1,0:T(8,128)} %mixing.1, f32[48,288]{1,0:T(8,128)} %damping.1, s32[32,64]{1,0:T(8,128)} %blocks.1), custom_call_target="tpu_custom_call" | custom-call | tf_op jit(solution)/shard_map/pallas_call | solution.py:798
  24.2 1.5 %shard_map.69 = (f32[2,16,48,288]{3,2,1,0:T(8,128)}, f32[48,288]{1,0:T(8,128)}) custom-call(f32[2,16,48,288]{3,2,1,0:T(8,128)S(1)} %get-tuple-element.4.tracer, f32[48,288]{1,0:T(8,128)S(1)} %get-tuple-element.5.surface), custom_call_target="tpu_custom_call" | custom-call | tf_op jit(solution)/shard_map/pallas_call | solution.py:800
